TPU v7x, 512 devices: a whole 4x4x16 slice. The times are simulated.
512 devices in a mesh: row: 32 (over y, x, core), col: 16 (over z).
Axes of the slice: x: 4, y: 4, z: 16, core: 2. Of those that a mesh axis runs over, the one named last changes fastest.
Arguments:
- inputs: float32 [262144, 128], P(('row', 'col')), may hold values from -6 to 6
- tasks: int32 [262144], P(('row', 'col')), may hold values from 0 to 7
- targets: float32 [262144], P(('row', 'col')), may hold values from -6 to 6
- inv_length: float32 [128], replicated, may hold values from 0.02 to 0.2
- task_factor: float32 [8, 8], replicated, may hold values from -2 to 2
- task_diag: float32 [8], replicated, may hold values from 0.3 to 1
- noise: float32 [8], replicated, may hold values from 0.05 to 0.5
- pivots: int32 [2, 64], replicated, may hold values from 0 to 262143, as said below
- test_inputs: float32 [16384, 128], P('row'), may hold values from -6 to 6
- test_tasks: int32 [16384], P('row'), may hold values from 0 to 7
Outputs:
- residual_diag: float32 [262144], P(('row', 'col'))
- lanczos_next: float32 [16384], P(('row', 'col'))
- test_coef: float32 [16384], P('row')
Inputs may be any that keep to these rules, and one draw needn't show every extreme that they name: `pivots`: all 128 pivot indices are distinct.
All inputs are finite; a program needn't handle non-finite values.
Results may differ from a plain program's by a relative error of at most 0.0003.
Values sent between devices are 32-bit elements; how exact they have to be, the bound alone decides.
A program may use at most 64 MiB of HBM per device.

v0:
```python
import math

import jax
import jax.numpy as jnp
from jax import lax
from jax.sharding import PartitionSpec as P

TASKS = 8
PIV = 64
SUB = 32


def right_solve(low, mat):
    return lax.linalg.triangular_solve(low, mat, left_side=False, lower=True, transpose_a=True)


def cho_apply(low, vec):
    column = vec[:, None]
    inner = lax.linalg.triangular_solve(low, column, left_side=True, lower=True)
    outer = lax.linalg.triangular_solve(low, inner, left_side=True, lower=True, transpose_a=True)
    return outer[:, 0]


def kernel_tile(a_rows, oh_rows, a_cols, oh_cols, task_cov):
    high = lax.Precision.HIGHEST
    sq_rows = jnp.sum(a_rows * a_rows, axis=1)
    sq_cols = jnp.sum(a_cols * a_cols, axis=1)
    cross = jnp.dot(a_rows, a_cols.T, precision=high)
    dist = sq_rows[:, None] + sq_cols[None, :] - 2.0 * cross
    scale = jnp.dot(jnp.dot(oh_rows, task_cov, precision=high), oh_cols.T, precision=high)
    return jnp.exp(-0.5 * dist) * scale


def pick_rows(values, local_idx, owned):
    return jnp.where(owned[:, None], values[local_idx], 0.0)


def per_device(
    inputs,
    tasks,
    targets,
    inv_length,
    task_factor,
    task_diag,
    noise,
    pivots,
    test_inputs,
    test_tasks,
):
    high = lax.Precision.HIGHEST
    task_cov = jnp.dot(task_factor, task_factor.T, precision=high) + jnp.diag(task_diag)
    scaled = inputs * inv_length[None, :]
    onehot = jax.nn.one_hot(tasks, TASKS, dtype=jnp.float32)
    rows_dev = inputs.shape[0]
    my_flat = lax.axis_index("row") * lax.axis_size("col") + lax.axis_index("col")
    first_piv = pivots[0]
    second_piv = pivots[1]
    owned_one = first_piv // rows_dev == my_flat
    local_one = first_piv % rows_dev
    owned_two = second_piv // rows_dev == my_flat
    local_two = second_piv % rows_dev
    a_one, oh_one = lax.psum(
        (pick_rows(scaled, local_one, owned_one), pick_rows(onehot, local_one, owned_one)),
        ("row", "col"),
    )
    lower_one = jnp.linalg.cholesky(kernel_tile(a_one, oh_one, a_one, oh_one, task_cov))
    first = right_solve(lower_one, kernel_tile(scaled, onehot, a_one, oh_one, task_cov))
    a_two, oh_two, first_two = lax.psum(
        (
            pick_rows(scaled, local_two, owned_two),
            pick_rows(onehot, local_two, owned_two),
            pick_rows(first, local_two, owned_two),
        ),
        ("row", "col"),
    )
    schur = kernel_tile(a_two, oh_two, a_two, oh_two, task_cov) - jnp.dot(
        first_two, first_two.T, precision=high
    )
    lower_two = jnp.linalg.cholesky(schur)
    cols_two = kernel_tile(scaled, onehot, a_two, oh_two, task_cov) - jnp.dot(
        first, first_two.T, precision=high
    )
    second = right_solve(lower_two, cols_two)
    bdiag = jnp.dot(onehot, jnp.diag(task_cov), precision=high)
    residual_diag = bdiag - jnp.sum(first * first, axis=1) - jnp.sum(second * second, axis=1)
    a_slab = scaled[:SUB]
    oh_slab = onehot[:SUB]
    factor_s = jnp.concatenate([first[:SUB], second[:SUB]], axis=1)
    y_slab = targets[:SUB]
    dvec = jnp.dot(oh_slab, noise, precision=high)
    inv_d = 1.0 / dvec
    gram, proj, yy = lax.psum(
        (
            jnp.dot(factor_s.T, inv_d[:, None] * factor_s, precision=high),
            jnp.dot(factor_s.T, y_slab * inv_d, precision=high),
            jnp.sum(y_slab * y_slab * inv_d),
        ),
        ("row", "col"),
    )
    cap = jnp.eye(2 * PIV, dtype=jnp.float32) + gram
    cap_low = jnp.linalg.cholesky(cap)
    cap_proj = cho_apply(cap_low, proj)
    zvec = (y_slab - jnp.dot(factor_s, cap_proj, precision=high)) * inv_d
    gamma = yy - jnp.sum(proj * cap_proj)
    qvec = zvec / jnp.sqrt(gamma)
    test_a = test_inputs * inv_length[None, :]
    test_oh = jax.nn.one_hot(test_tasks, TASKS, dtype=jnp.float32)
    test_zero = jnp.zeros((test_a.shape[0],), jnp.float32)
    rows_a, rows_oh = (
        lax.all_gather(a_slab, "col", axis=0, tiled=True),
        lax.all_gather(oh_slab, "col", axis=0, tiled=True),
    )
    start_carry = (jnp.zeros((rows_a.shape[0],), jnp.float32), test_zero)
    piece_a = lax.all_gather(a_slab, "row", axis=0, tiled=True)
    piece_oh = lax.all_gather(oh_slab, "row", axis=0, tiled=True)
    piece_q = lax.all_gather(qvec, "row", axis=0, tiled=True)
    width = math.gcd(piece_a.shape[0], 512)

    def step(idx, acc):
        col_a = lax.dynamic_slice_in_dim(piece_a, idx * width, width, 0)
        col_oh = lax.dynamic_slice_in_dim(piece_oh, idx * width, width, 0)
        col_q = lax.dynamic_slice_in_dim(piece_q, idx * width, width, 0)
        slab_part = jnp.dot(
            kernel_tile(rows_a, rows_oh, col_a, col_oh, task_cov), col_q, precision=high
        )
        test_part = jnp.dot(
            kernel_tile(test_a, test_oh, col_a, col_oh, task_cov), col_q, precision=high
        )
        return (acc[0] + slab_part, acc[1] + test_part)

    slab_partial, test_partial = lax.fori_loop(0, piece_a.shape[0] // width, step, start_carry)
    kprod = lax.psum_scatter(slab_partial, "col", scatter_dimension=0, tiled=True)
    kq = lax.psum(test_partial, "col")
    wvec = kprod + dvec * qvec
    alpha, back = lax.psum(
        (jnp.sum(qvec * wvec), jnp.dot(factor_s.T, wvec * inv_d, precision=high)), ("row", "col")
    )
    lanczos_next = (
        wvec - jnp.dot(factor_s, cho_apply(cap_low, back), precision=high)
    ) * inv_d - alpha * qvec
    test_coef = kq / jnp.sqrt(alpha)
    return (residual_diag, lanczos_next, test_coef)


def solution(mesh):
    return jax.shard_map(
        per_device,
        mesh=mesh,
        in_specs=(
            P(("row", "col"), None),
            P(("row", "col")),
            P(("row", "col")),
            P(),
            P(),
            P(),
            P(),
            P(),
            P("row", None),
            P("row"),
        ),
        out_specs=(P(("row", "col")), P(("row", "col")), P("row")),
        check_vma=False,
    )
```

profile of v0, /device:TPU:1, one launch (start us, length us, event | category | flops | bytes accessed | tf_op | source)
XLA Modules:
  0.0 932.3 jit_solution(5498400900286640022)
XLA Ops:
  7.2 0.9 iota_compare_fusion.1
  8.1 0.8 fusion.66
  8.9 0.6 gather_fusion.4
  9.8 0.6 gather_fusion.3
  10.4 0.6 gather_fusion.2
  11.0 0.6 gather_fusion.1
  11.8 0.6 copy-done.6
  12.6 0.7 copy-done.5
  13.7 111.3 %all-reduce.5 = (f32[64,8]{1,0:T(8,128)S(1)}, f32[64,128]{1,0:T(8,128)S(1)}) all-reduce(f32[64,8]{1,0:T(8,128)S(1)} %broadcast_select_fusion.2, f32[64,128]{1,0:T(8,128)S(1)} %broadcast_select_fusion.4), channel_id=1, replica_groups=mesh['row'=32,'col'=16] {'row','col'}, use_global_device_ids=true, to_apply=%region_2.3 | all-reduce | flops 8704 | bytes 69632 | tf_op jit(solution)/shard_map/psum | solution.py:62
  126.0 5.8 cholesky.86
  131.9 0.6 compare_reduce_fusion.1
  132.5 0.7 fusion.52
  133.2 4.9 custom-call.21
  138.1 0.5 fusion.25
  138.5 0.3 multiply_reduce_fusion.5
  139.0 0.6 gather_fusion.5
  139.7 99.1 %all-reduce.4 = (f32[64,8]{1,0:T(8,128)S(1)}, f32[64,128]{1,0:T(8,128)S(1)}, f32[64,64]{1,0:T(8,128)S(1)}) all-reduce(f32[64,8]{1,0:T(8,128)S(1)} %broadcast_select_fusion.1, f32[64,128]{1,0:T(8,128)S(1)} %broadcast_select_fusion.3, f32[64,64]{1,0:T(8,128)S(1)} %broadcast_select_fusion), channel_id=1, replica_groups=mesh['row'=32,'col'=16] {'row','col'}, use_global_device_ids=true, to_apply=%region_9.12 | all-reduce | flops 12800 | bytes 102400 | tf_op jit(solution)/shard_map/psum | solution.py:68
  239.6 0.4 fusion.21
  240.8 5.8 cholesky.97
  246.7 0.6 compare_reduce_fusion
  247.3 0.7 fusion.53
  248.0 4.9 custom-call.22
  252.9 0.4 multiply_reduce_fusion.4
  253.5 0.6 copy-done.4
  254.1 0.8 multiply_reduce_fusion.9
  254.9 0.9 fusion.58
  255.8 22.6 %all_gather.15 = f32[512,128]{1,0:T(8,128)S(1)} all-gather(f32[32,128]{1,0:T(8,128)S(1)} %slice.59), channel_id=1, replica_groups=mesh['row'=32,'col'=16] {'col'}, dimensions={0}, use_global_device_ids=true | all-gather | bytes 278528 | tf_op jit(solution)/shard_map/all_gather | solution.py:110
  278.5 31.1 %all_gather.16 = f32[1024,128]{1,0:T(8,128)S(1)} all-gather(f32[32,128]{1,0:T(8,128)S(1)} %slice.59), channel_id=1, replica_groups=mesh['row'=32,'col'=16] {'row'}, dimensions={0}, use_global_device_ids=true | all-gather | bytes 540672 | tf_op jit(solution)/shard_map/all_gather | solution.py:114
  309.6 0.6 gather_fusion
  310.2 0.3 fusion.41
  310.7 19.6 %all-gather.1 = f32[16,32,8]{1,2,0:T(8,128)S(1)} all-gather(f32[1,32,8]{1,2,0:T(8,128)S(1)} %copy.54), channel_id=1, replica_groups=mesh['row'=32,'col'=16] {'col'}, dimensions={0}, use_global_device_ids=true | all-gather | bytes 17408 | tf_op jit(solution)/shard_map/all_gather | solution.py:111
  330.7 0.5 copy-done.8
  331.5 0.6 subtract_subtract_fusion
  332.2 29.6 %all-gather = f32[32,32,8]{1,2,0:T(8,128)S(1)} all-gather(f32[1,32,8]{1,2,0:T(8,128)S(1)} %copy.54), channel_id=1, replica_groups=mesh['row'=32,'col'=16] {'row'}, dimensions={0}, use_global_device_ids=true | all-gather | bytes 33792 | tf_op jit(solution)/shard_map/all_gather | solution.py:115
  362.0 1.3 dynamic-slice
  363.9 1.3 dynamic-slice.1
  365.9 100.9 %all-reduce.3 = (f32[128]{0:T(128)S(1)}, f32[]{:T(128)}) all-reduce(f32[128]{0:T(128)S(1)} %convolution_bitcast_fusion.10, f32[]{:T(128)} %get-tuple-element.379), channel_id=1, replica_groups=mesh['row'=32,'col'=16] {'row','col'}, use_global_device_ids=true, to_apply=%region_15.18 | all-reduce | flops 129 | bytes 1032 | tf_op jit(solution)/shard_map/psum | solution.py:92
  466.8 223.5 %all-reduce.9.cloned.1.call-done = f32[128,128]{1,0:T(8,128)} async-done(((f32[128,128]{1,0:T(8,128)}), f32[128,128]{1,0:T(8,128)}) %all-reduce.9.cloned.1.call-update) | async-done | bytes 65552 | tf_op jit(solution)/shard_map/psum | solution.py:92
  690.3 0.9 convert_add_fusion
  691.3 0.7 copy-done.1
  692.1 11.7 %cholesky.47 = f32[128,128]{1,0:T(8,128)S(1)} custom-call(f32[128,128]{1,0:T(8,128)S(1)} %fusion.51), custom_call_target="Cholesky" | custom-call | tf_op jit(solution)/shard_map/jit(cholesky)/cholesky | solution.py:101
  703.8 0.6 compare_reduce_fusion.2
  704.4 0.7 fusion.45
  705.1 9.8 %custom-call.24 = f32[1,128,128]{1,2,0:T(8,128)S(1)} custom-call(f32[1,128,128]{2,1,0:T(8,128)S(1)} %fusion.45), custom_call_target="InvertDiagBlocksLowerTriangular" | custom-call | tf_op jit(solution)/shard_map/triangular_solve/custom-call.4 | solution.py:20
  715.1 0.8 fusion.70
  717.6 62.6 %all-reduce = f32[1024]{0:T(1024)S(1)} all-reduce(f32[1024]{0:T(1024)S(1)} %dynamic-update-slice.5), channel_id=1, replica_groups=mesh['row'=32,'col'=16] {'row'}, use_global_device_ids=true, to_apply=%add | all-reduce | flops 1024 | bytes 8192
  780.3 11.9 %while.18 = (s32[]{:T(128)}, f32[512]{0:T(512)S(1)}, f32[512]{0:T(512)S(1)}, f32[512]{0:T(512)S(1)}, f32[1024,128]{1,0:T(8,128)S(1)}, /*index=5*/f32[512,128]{1,...) while((s32[]{:T(128)}, f32[512]{0:T(512)S(1)}, ...), condition=%wide.region_23.28_spmd.clone, body=%wide.region_21.27_spmd.clone.sunk | while | flops 864683520 | bytes 9799917 | solution.py:131
  780.4 1.1 fusion.164
  781.6 1.0 fusion.165
  782.7 0.6 fusion.166
  783.4 1.1 fusion.167
  784.5 1.0 fusion.168
  785.6 0.6 fusion.169
  786.4 1.1 fusion.164
  787.5 1.0 fusion.165
  788.7 0.6 fusion.166
  789.3 1.1 fusion.167
  790.5 1.0 fusion.168
  791.5 0.6 fusion.169
  792.2 20.1 %all-reduce.6 = (f32[512]{0:T(512)S(1)}, f32[512]{0:T(512)S(1)}) all-reduce(f32[512]{0:T(512)S(1)} %get-tuple-element.275, f32[512]{0:T(512)S(1)} %get-tuple-element.276), channel_id=2, replica_groups=mesh['row'=32,'col'=16] {'col'}, use_global_device_ids=true, to_apply=%region_24.29.clone | all-reduce | flops 1024 | bytes 8192
  812.3 0.7 multiply_reduce_fusion.8
  813.1 109.4 %all-reduce.2 = (f32[128,1]{0,1:T(1,128)S(1)}, f32[]{:T(128)}) all-reduce(f32[128,1]{0,1:T(1,128)S(1)} %convolution_bitcast_fusion.7, f32[]{:T(128)} %get-tuple-element.375), channel_id=1, replica_groups=mesh['row'=32,'col'=16] {'row','col'}, use_global_device_ids=true, to_apply=%region_25.30 | all-reduce | flops 129 | bytes 1032 | tf_op jit(solution)/shard_map/psum | solution.py:135
  923.5 1.3 fusion.37
  924.8 0.6 broadcast_divide_fusion
  (83 shorter events, 6.9 us)
Async XLA Ops:
  7.2 4.4 copy-start
  7.2 683.2 %all-reduce.9.cloned.1.call-start = ((), (), s32[]{:S(2)}) async-start(), calls=%async_computation | async-start | bytes 131072 | tf_op jit(solution)/shard_map/psum | solution.py:92
  7.2 2.3 copy-start.2
  7.2 2.3 copy-start.3
  8.9 0.7 copy-start.7
  11.0 0.7 copy-start.9
  11.6 0.7 copy-start.6
  12.6 0.7 copy-start.5
  253.4 0.7 copy-start.4
  253.5 0.7 copy-start.10
  330.5 0.7 copy-start.8
  691.2 0.8 copy-start.1
Sparse Core Ops, SparseCore 0:
  255.9 434.3 all-reduce.8
where the time goes:
time: 934 us; the launch traced here: 932 us
  blocking collectives  606 us (65%)
  waiting for transfers between devices  224 us (24%)
  other arithmetic  52.8 us (6%)
  matrix products  20.9 us (2%)
  between operations  17.8 us (2%)
  local copies, waits for them, and re-layouts  10.6 us (1%)
    psum x1, waiting for transfers between devices, per_device(): lax.psum((jnp.dot(factor_s.T, inv_d[:, None] * factor_s, precision=high),...  224 us
    psum x1, blocking collectives, per_device(): lax.psum((pick_rows(scaled, local_one, owned_one), pick_rows(onehot, loca...  111 us
    psum x1, blocking collectives, per_device(): lax.psum((jnp.sum(qvec * wvec), jnp.dot(factor_s.T, wvec * inv_d, precisi...  109 us
    psum x1, blocking collectives, per_device(): lax.psum((jnp.dot(factor_s.T, inv_d[:, None] * factor_s, precision=high),...  101 us
    psum x1, blocking collectives, per_device(): lax.psum((pick_rows(scaled, local_two, owned_two), pick_rows(onehot, loca...  99.1 us
    unnamed x2, blocking collectives  82.7 us
    all_gather x1, blocking collectives, per_device(): piece_a = lax.all_gather(a_slab, 'row', axis=0, tiled=True)  31.1 us
    all_gather x1, blocking collectives, per_device(): piece_oh = lax.all_gather(oh_slab, 'row', axis=0, tiled=True)  29.6 us
  transfers between devices with their start and end apart: 1, of which 1 were waited for; matrix products, arithmetic and copies ran while one was open for 1% of the time, Pallas kernels for 0%

commit v1 on v0

v1 whole, which is shorter than its diff:
```python
import functools

import jax
import jax.numpy as jnp
from jax import lax
from jax.experimental import pallas as pl
from jax.experimental.pallas import tpu as pltpu
from jax.sharding import PartitionSpec as P

TASKS = 8
PIV = 64
NP = 2 * PIV
SUB = 32
LANES = 128
HIGH = lax.Precision.HIGHEST
MESH = pl.DeviceIdType.MESH
F32 = jnp.float32

RS1, Z1, AG1, SLC, SLR, Z2, AG2, Z3, P3 = range(9)


def iota(shape, axis):
    return lax.broadcasted_iota(jnp.int32, shape, axis)


def mm(a, b, precision=HIGH):
    return lax.dot_general(a, b, (((1,), (0,)), ((), ())), precision=precision, preferred_element_type=F32)


def mm_nt(a, b, precision=HIGH):
    return lax.dot_general(a, b, (((1,), (1,)), ((), ())), precision=precision, preferred_element_type=F32)


def diag_to_row(col, eye):
    return jnp.sum(jnp.where(eye, col, 0.0), axis=0, keepdims=True)


def row_to_col(row, eye):
    return jnp.sum(jnp.where(eye, row, 0.0), axis=1, keepdims=True)


def onehot_rows(task_row):
    n = task_row.shape[1]
    return (iota((TASKS, n), 0).astype(F32) == task_row).astype(F32)


def half_sq_row(a):
    ones = jnp.full((8, a.shape[1]), 0.5, F32)
    return mm_nt(ones, a * a)[0:1, :]


def eliminate(a, lane):
    top = a[0:8, :]
    cols = [jnp.broadcast_to(top[:, m : m + 1], (8, LANES)) for m in range(8)]
    d = [[cols[m][i : i + 1, :] for m in range(8)] for i in range(8)]
    rows = [jnp.where(lane < 8, (lane == i).astype(F32), top[i : i + 1, :]) for i in range(8)]
    for m in range(8):
        inv = 1.0 / d[m][m]
        rows[m] = rows[m] * inv
        for j in range(m + 1, 8):
            d[m][j] = d[m][j] * inv
        for i in range(8):
            if i != m:
                f = d[i][m]
                rows[i] = rows[i] - f * rows[m]
                for j in range(m + 1, 8):
                    d[i][j] = d[i][j] - f * d[m][j]
    body = a[8:, :]
    acc = jnp.where(lane < 8, 0.0, body)
    for m in range(8):
        acc = acc - body[:, m : m + 1] * rows[m]
    out = jnp.concatenate([acc] + rows, axis=0)
    return pltpu.roll(out, LANES - 8, axis=1)


def kernel(
    nr, nc,
    pivots, tasks_s, inputs, tasks, targets, il, tfac, tdiag, noise, tests, ttasks,
    res_o, ln_o, tc_o,
    psrc, rsbuf, zsrc1, zbuf1, apiv, agsrc1, slsrc, bufc, bufr,
    zsrc2, zbuf2, agsrc2, gram, zsrc3, zbuf3, psrc3, pbuf3,
    art, kmat, gt_c, gt_r, kp_own, mmat, pmat,
    ssem, rsem,
):
    r = lax.axis_index("row")
    c = lax.axis_index("col")
    me = r * nc + c
    chunks = nr // 2
    cr = NP // chunks
    mine = r // 2
    rows_dev = inputs.shape[0]
    nown = rows_dev // LANES
    ntest = tests.shape[0] // LANES
    nrr = nc * SUB
    ncc = nr * SUB
    prr, pcc = nrr // LANES, ncc // LANES

    def in_row(k):
        return lax.rem(r + k, nr)

    def in_col(k):
        return lax.rem(c + k, nc)

    order_z = sorted(range(1, nc), key=lambda k: -min(k, nc - k))
    order_p = list(range(1, nr))

    bar = pltpu.get_barrier_semaphore()
    for k in order_z:
        pl.semaphore_signal(bar, inc=1, device_id={"row": r, "col": in_col(k)}, device_id_type=MESH)
    for k in order_p:
        pl.semaphore_signal(bar, inc=1, device_id={"row": in_row(k), "col": c}, device_id_type=MESH)

    def send_z(src, dst, sem):
        for k in order_z:
            pltpu.make_async_remote_copy(
                src, dst, ssem.at[sem], rsem.at[sem], device_id={"row": r, "col": in_col(k)}, device_id_type=MESH
            ).start()

    def send_p(src_of, dst, sem, step=1):
        for k in order_p:
            if k % step == 0:
                to = in_row(k)
                pltpu.make_async_remote_copy(
                    src_of(to), dst, ssem.at[sem], rsem.at[sem], device_id={"row": to, "col": c}, device_id_type=MESH
                ).start()

    def wait(ref, sem):
        pltpu.make_async_copy(ref, ref, sem).wait()

    lane = iota((1, LANES), 1)
    eye8 = iota((TASKS, TASKS), 0) == iota((TASKS, TASKS), 1)
    eye = iota((NP, NP), 0) == iota((NP, NP), 1)
    scale = il[...]
    cov = mm_nt(tfac[...], tfac[...]) + jnp.where(eye8, jnp.broadcast_to(tdiag[...], (TASKS, TASKS)), 0.0)
    noise_col = row_to_col(jnp.broadcast_to(noise[...], (TASKS, TASKS)), eye8)

    def pick(i, trow):
        piv = pivots[i // PIV, lax.rem(i, PIV)]
        own = (piv // rows_dev == me).astype(F32)
        loc = lax.rem(piv, rows_dev)
        row = inputs[pl.ds(loc, 1), :] * scale * own
        psrc[i // cr, pl.ds(lax.rem(i, cr), 1), :] = row
        return trow + jnp.where(lane == i, tasks_s[loc].astype(F32) * own, 0.0)

    trow = lax.fori_loop(0, NP, pick, jnp.zeros((1, LANES), F32))
    for j in range(chunks):
        psrc[j, cr : cr + 1, :] = trow

    slsrc[0:SUB, :] = inputs[0:SUB, :] * scale
    t_own = tasks[0:1, 0:SUB].astype(F32)
    y_own = targets[0:1, 0:SUB]
    t4 = jnp.concatenate([t_own] * 4, axis=1)
    y4 = jnp.concatenate([y_own] * 4, axis=1)
    at_r = lane // SUB == lax.rem(r, 4)
    at_c = lane // SUB == lax.rem(c, 4)
    slsrc[SUB : SUB + 1, :] = jnp.where(at_r, t4, 0.0)
    slsrc[SUB + 1 : SUB + 2, :] = jnp.where(at_r, y4, 0.0)
    slsrc[SUB + 2 : SUB + 3, :] = jnp.where(at_c, t4, 0.0)
    slsrc[SUB + 3 : SUB + 4, :] = jnp.where(at_c, y4, 0.0)
    bufc[r] = slsrc[...]
    bufr[c] = slsrc[...]
    rsbuf[r] = psrc[mine]
    art[nrr:, :] = tests[...] * scale

    pl.semaphore_wait(bar, nr - 1 + nc - 1)

    send_p(lambda to: psrc.at[to // 2], rsbuf.at[r], RS1)
    wait(rsbuf.at[pl.ds(0, nr - 1)], rsem.at[RS1])
    part = rsbuf[0]
    for k in range(1, nr):
        part = part + rsbuf[k]
    zsrc1[...] = part
    zbuf1[c] = part
    send_z(zsrc1, zbuf1.at[c], Z1)
    send_p(lambda to: slsrc, bufc.at[r], SLC)
    wait(zbuf1.at[pl.ds(0, nc - 1)], rsem.at[Z1])
    part = zbuf1[0]
    for k in range(1, nc):
        part = part + zbuf1[k]
    agsrc1[...] = part[0:cr, :]
    my_rows = pl.ds(pl.multiple_of(mine * cr, cr), cr)
    apiv[my_rows, :] = part[0:cr, :]
    trow = part[cr : cr + 1, :]
    send_p(lambda to: agsrc1, apiv.at[my_rows], AG1, step=2)
    send_z(slsrc, bufr.at[c], SLR)

    wait(bufc.at[pl.ds(0, nr - 1)], rsem.at[SLC])

    def pieces(buf, n, at):
        out = []
        for k in range(n):
            row = buf[4 * k, at : at + 1, :]
            for s in range(1, 4):
                row = row + buf[4 * k + s, at : at + 1, :]
            out.append(row)
        return out

    ohc = onehot_rows(jnp.concatenate(pieces(bufc, pcc, SUB), axis=1))
    y_c = jnp.concatenate(pieces(bufc, pcc, SUB + 1), axis=1)
    di_c = 1.0 / jnp.sum(ohc * noise_col, axis=0, keepdims=True)
    a_c = bufc[:, 0:SUB, :].reshape(ncc, LANES)
    hs_c = half_sq_row(a_c)
    ohp_t = onehot_rows(trow)
    t_col = row_to_col(jnp.broadcast_to(trow, (NP, NP)), eye)
    ohp = (iota((NP, TASKS), 1).astype(F32) == t_col).astype(F32)
    covp = mm(ohp, cov)

    n_ag = chunks - 1
    wait(apiv.at[pl.ds(0, n_ag * cr)], rsem.at[AG1])
    ap = apiv[...]
    hs_p = 0.5 * jnp.sum(ap * ap, axis=1, keepdims=True)

    def tile_p(a, hs, oh):
        return jnp.exp(mm_nt(ap, a) - hs_p - hs) * mm(covp, oh)

    pm = tile_p(ap, half_sq_row(ap), ohp_t)
    pmat[...] = pm
    nu = 1.0 / jnp.max(jnp.sum(jnp.abs(pm), axis=0, keepdims=True), axis=1, keepdims=True)
    eye_f = eye.astype(F32)
    fast = lax.Precision.DEFAULT
    w = (2.0 * eye_f - pm * nu) * nu
    for _ in range(3):
        w = mm(w, 2.0 * eye_f - mm(pm, w, fast), fast)
    w_t = w.T
    gtc = mm(w_t, tile_p(a_c, hs_c, ohc))
    gt_c[...] = gtc
    g_row = y_c * di_c
    left = jnp.concatenate([gt_c[my_rows, :] * di_c, jnp.broadcast_to(g_row, (8, ncc))], axis=0)
    bg = mm_nt(left, gtc)
    yy = jnp.sum(g_row * y_c, axis=1, keepdims=True)
    part = jnp.concatenate([bg[0 : cr + 1, :], jnp.broadcast_to(yy, (1, LANES))], axis=0)
    zsrc2[...] = part
    zbuf2[c] = part

    send_z(zsrc2, zbuf2.at[c], Z2)
    wait(bufr.at[pl.ds(0, nc - 1)], rsem.at[SLR])
    art[0:nrr, :] = bufr[:, 0:SUB, :].reshape(nrr, LANES)
    ohr = onehot_rows(jnp.concatenate(pieces(bufr, prr, SUB + 2), axis=1))
    y_r = jnp.concatenate(pieces(bufr, prr, SUB + 3), axis=1)
    d_r = jnp.sum(ohr * noise_col, axis=0, keepdims=True)
    di_r = 1.0 / d_r
    oht = onehot_rows(jnp.concatenate([ttasks[k : k + 1, :].astype(F32) for k in range(ntest)], axis=1))
    cov_rt = mm(cov, jnp.concatenate([ohr, oht], axis=1))
    a_rt = art[...]
    hs_rt = half_sq_row(a_rt)

    def k_chunk(k):
        a = bufc[4 * k : 4 * k + 4, 0:SUB, :].reshape(LANES, LANES)
        hs = 0.5 * jnp.sum(a * a, axis=1, keepdims=True)
        oh = jnp.transpose(ohc[:, k * LANES : (k + 1) * LANES])
        kmat[k * LANES : (k + 1) * LANES, :] = jnp.exp(mm_nt(a, a_rt) - hs - hs_rt) * mm(oh, cov_rt)

    for k in range(pcc):
        k_chunk(k)

    wait(zbuf2.at[pl.ds(0, nc - 1)], rsem.at[Z2])
    part = zbuf2[0]
    for k in range(1, nc):
        part = part + zbuf2[k]
    agsrc2[...] = part[0:cr, :]
    gram[my_rows, :] = part[0:cr, :]
    g = part[cr : cr + 1, :]
    yy = part[cr + 1 : cr + 2, :]
    send_p(lambda to: agsrc2, gram.at[my_rows], AG2, step=2)
    gt_r[...] = mm(w_t, tile_p(art[0:nrr, :], hs_rt[:, 0:nrr], ohr))
    a_own = inputs[...] * scale
    oho = onehot_rows(jnp.concatenate([tasks[k : k + 1, :].astype(F32) for k in range(nown)], axis=1))
    kp_own[...] = tile_p(a_own, half_sq_row(a_own), oho)
    base = mm(mm(w_t, pm), w)
    wait(gram.at[pl.ds(0, n_ag * cr)], rsem.at[AG2])
    mmat[...] = base + gram[...]

    def gj(_, carry):
        mmat[...] = eliminate(mmat[...], lane)
        pmat[...] = eliminate(pmat[...], lane)
        return carry

    lax.fori_loop(0, NP // 8, gj, 0)
    minv = mmat[...]
    x_col = jnp.sum(minv * g, axis=1, keepdims=True)
    x_row = diag_to_row(x_col, eye)
    gamma = yy[:, 0:1] - jnp.sum(g * x_row, axis=1, keepdims=True)
    rg = 1.0 / jnp.sqrt(gamma)
    q_c = (y_c - jnp.sum(gt_c[...] * x_col, axis=0, keepdims=True)) * di_c * rg
    q_r = (y_r - jnp.sum(gt_r[...] * x_col, axis=0, keepdims=True)) * di_r * rg
    q8 = jnp.concatenate(
        [q_c[:, k * LANES : (k + 1) * LANES] for k in range(pcc)] + [jnp.zeros((8 - pcc, LANES), F32)] * (pcc < 8), axis=0
    )
    qt = jnp.transpose(q8)
    acc = jnp.zeros((1, kmat.shape[1]), F32)
    for k in range(pcc):
        acc = acc + jnp.sum(kmat[k * LANES : (k + 1) * LANES, :] * qt[:, k : k + 1], axis=0, keepdims=True)
    for k in range(prr + ntest):
        zsrc3[k : k + 1, :] = acc[:, k * LANES : (k + 1) * LANES]

    send_z(zsrc3, zbuf3.at[c], Z3)
    zbuf3[c] = zsrc3[...]
    kp = kp_own[...]
    cov_d = jnp.sum(jnp.where(eye8, cov, 0.0), axis=1, keepdims=True)
    res = jnp.sum(oho * cov_d, axis=0, keepdims=True) - jnp.sum(mm(pmat[...], kp) * kp, axis=0, keepdims=True)
    for k in range(nown):
        res_o[k : k + 1, :] = res[:, k * LANES : (k + 1) * LANES]
    wait(zbuf3.at[pl.ds(0, nc - 1)], rsem.at[Z3])
    part = zbuf3[0]
    for k in range(1, nc):
        part = part + zbuf3[k]
    w_r = jnp.concatenate([part[k : k + 1, :] for k in range(prr)], axis=1) + d_r * q_r
    kq = part[prr:, :]
    gtr = gt_r[...]
    back = diag_to_row(jnp.sum(gtr * (w_r * di_r), axis=1, keepdims=True), eye)
    alpha = jnp.sum(w_r * q_r, axis=1, keepdims=True)
    part = jnp.concatenate([back, jnp.broadcast_to(alpha, (1, LANES))], axis=0)
    psrc3[...] = part
    pbuf3[r] = part
    send_p(lambda to: psrc3, pbuf3.at[r], P3)
    wait(pbuf3.at[pl.ds(0, nr - 1)], rsem.at[P3])
    part = pbuf3[0]
    for k in range(1, nr):
        part = part + pbuf3[k]
    alpha = part[1:2, 0:1]
    b_col = jnp.sum(minv * part[0:1, :], axis=1, keepdims=True)
    ln = (w_r - jnp.sum(gtr * b_col, axis=0, keepdims=True)) * di_r - alpha * q_r
    out = jnp.zeros((1, SUB), F32)
    for k in range(nc):
        out = out + jnp.where(c == k, ln[:, k * SUB : (k + 1) * SUB], 0.0)
    ln_o[...] = out
    tc_o[...] = kq * (1.0 / jnp.sqrt(alpha))

    wait(rsbuf.at[pl.ds(0, nr - 1)], ssem.at[RS1])
    wait(zbuf1.at[pl.ds(0, nc - 1)], ssem.at[Z1])
    wait(apiv.at[pl.ds(0, n_ag * cr)], ssem.at[AG1])
    wait(bufc.at[pl.ds(0, nr - 1)], ssem.at[SLC])
    wait(bufr.at[pl.ds(0, nc - 1)], ssem.at[SLR])
    wait(zbuf2.at[pl.ds(0, nc - 1)], ssem.at[Z2])
    wait(gram.at[pl.ds(0, n_ag * cr)], ssem.at[AG2])
    wait(zbuf3.at[pl.ds(0, nc - 1)], ssem.at[Z3])
    wait(pbuf3.at[pl.ds(0, nr - 1)], ssem.at[P3])


def per_device(
    nr, nc, inputs, tasks, targets, inv_length, task_factor, task_diag, noise, pivots, test_inputs, test_tasks
):
    rows_dev = inputs.shape[0]
    test_dev = test_inputs.shape[0]
    nown, ntest = rows_dev // LANES, test_dev // LANES
    chunks = nr // 2
    cr = NP // chunks
    nrr, ncc = nc * SUB, nr * SUB
    prr = nrr // LANES
    vmem = pl.BlockSpec(memory_space=pltpu.VMEM)
    smem = pl.BlockSpec(memory_space=pltpu.SMEM)

    def buf(*shape):
        return pltpu.VMEM(shape, F32)

    res, ln, tc = pl.pallas_call(
        functools.partial(kernel, nr, nc),
        out_shape=(
            jax.ShapeDtypeStruct((nown, LANES), F32),
            jax.ShapeDtypeStruct((1, SUB), F32),
            jax.ShapeDtypeStruct((ntest, LANES), F32),
        ),
        in_specs=[smem, smem] + [vmem] * 9,
        out_specs=(vmem, vmem, vmem),
        scratch_shapes=[
            buf(chunks, cr + 1, LANES), buf(nr, cr + 1, LANES), buf(cr + 1, LANES), buf(nc, cr + 1, LANES),
            buf(NP, LANES), buf(cr, LANES), buf(SUB + 4, LANES), buf(nr, SUB + 4, LANES), buf(nc, SUB + 4, LANES),
            buf(cr + 2, LANES), buf(nc, cr + 2, LANES), buf(cr, LANES), buf(NP, LANES),
            buf(prr + ntest, LANES), buf(nc, prr + ntest, LANES), buf(2, LANES), buf(nr, 2, LANES),
            buf(nrr + test_dev, LANES), buf(ncc, nrr + test_dev), buf(NP, ncc), buf(NP, nrr), buf(NP, rows_dev),
            buf(NP, NP), buf(NP, NP),
            pltpu.SemaphoreType.DMA((9,)), pltpu.SemaphoreType.DMA((9,)),
        ],
        compiler_params=pltpu.CompilerParams(
            collective_id=0, has_side_effects=True, vmem_limit_bytes=40 * 1024 * 1024
        ),
    )(
        pivots, tasks, inputs, tasks.reshape(nown, LANES), targets.reshape(nown, LANES), inv_length[None, :],
        task_factor, task_diag[None, :], noise[None, :], test_inputs, test_tasks.reshape(ntest, LANES),
    )
    return res.reshape(rows_dev), ln.reshape(SUB), tc.reshape(test_dev)


def solution(mesh):
    both = ("row", "col")
    return jax.shard_map(
        functools.partial(per_device, mesh.shape["row"], mesh.shape["col"]),
        mesh=mesh,
        in_specs=(P(both, None), P(both), P(both), P(), P(), P(), P(), P(), P("row", None), P("row")),
        out_specs=(P(both), P(both), P("row")),
        check_vma=False,
    )
```

time: 934 us -> 89 us (0.10)
  blocking collectives: 606 us -> 0 us
  waiting for transfers between devices: 224 us -> 0 us
  Pallas kernels: 0 us -> 81.8 us
  other arithmetic: 52.8 us -> 0 us
  matrix products: 20.9 us -> 0 us
  between operations: 17.8 us -> 0.69 us
    psum x4 -> x0, blocking collectives: 421 us -> none  [the longest x1 111 us: per_device(): lax.psum((pick_rows(scaled, local_one, owned_one), pick_rows(onehot, loca...]
    psum x1 -> x0, waiting for transfers between devices: 224 us -> none  [per_device(): lax.psum((jnp.dot(factor_s.T, inv_d[:, None] * factor_s, precision=high),...]
    all_gather x4 -> x0, blocking collectives: 103 us -> none  [the longest x1 31.1 us: per_device(): piece_a = lax.all_gather(a_slab, 'row', axis=0, tiled=True)]
    unnamed x2 -> x0, blocking collectives: 82.7 us -> none
    pallas_call x0 -> x1, Pallas kernels: none -> 81.8 us  [per_device(): pl.pallas_call(functools.partial(kernel, nr, nc), out_shape=(jax.ShapeDty...]
    another operation x15 -> x0, other arithmetic: 47 us -> none  [the longest x3 12.4 us: per_device(): cap_low = jnp.linalg.cholesky(cap)]
    dot_general x35 -> x0, matrix products: 18.9 us -> none  [the longest x8 5.87 us: kernel_tile(): cross = jnp.dot(a_rows, a_cols.T, precision=high)]
  transfers between devices with their start and end apart: 1 -> 0, of which waited for: 1 -> 0; matrix products, arithmetic and copies ran while one was open for 1% -> 0% of each run, Pallas kernels for 0% -> 0%
where the time goes in v1:
time: 89 us; the launch traced here: 88.7 us
  Pallas kernels  81.8 us (92%)
  local copies, waits for them, and re-layouts  6.24 us (7%)
    pallas_call x1, Pallas kernels, per_device(): pl.pallas_call(functools.partial(kernel, nr, nc), out_shape=(jax.ShapeDty...  81.8 us
    unnamed x23, local copies, waits for them, and re-layouts  6.24 us

profile of v1, /device:TPU:1, one launch (start us, length us, event | category | flops | bytes accessed | tf_op | source)
XLA Modules:
  0.0 88.7 jit_solution(10102733014057481349)
XLA Ops:
  0.6 0.0 copy-start.5
  0.6 0.0 copy-start.4
  0.7 0.0 copy-start.3
  0.7 0.0 copy-start.2
  0.7 0.0 copy-start.6
  0.7 0.6 copy-done.5
  1.3 0.0 copy-done.4
  1.3 0.0 copy-done.3
  1.4 0.0 copy-done.2
  1.4 0.0 copy-done.6
  1.4 0.0 copy-start
  1.4 0.9 %copy-done = f32[512,128]{1,0:T(8,128)S(1)} copy-done((f32[512,128]{1,0:T(8,128)S(1)}, f32[512,128]{1,0:T(8,128)}, u32[]{:S(2)}) %copy-start) | copy-done | bytes 262168
  2.3 0.0 copy-start.1
  2.3 0.9 %copy-done.1 = f32[512,128]{1,0:T(8,128)S(1)} copy-done((f32[512,128]{1,0:T(8,128)S(1)}, f32[512,128]{1,0:T(8,128)}, u32[]{:S(2)}) %copy-start.1) | copy-done | bytes 262168
  3.3 0.0 copy-start.7
  3.3 0.7 copy-done.7
  3.9 0.0 copy-start.8
  3.9 0.7 copy-done.8
  4.6 0.0 copy-start.9
  4.6 0.7 copy-done.9
  5.2 81.8 %shard_map.121 = (f32[4,128]{1,0:T(4,128)S(1)}, f32[1,32]{1,0:T(1,128)S(1)}, f32[4,128]{1,0:T(4,128)S(1)}) custom-call(s32[2,64]{1,0:T(2,128)S(1)} %copy-done.6, s32[512]{0:T(512)S(1)} %copy-done.2, f32[512,128]{1,0:T(8,128)S(1)} %copy-done, s32[4,128]{1,0:T(4,128)S(1)} %bitcast.9, f32[4,128]{1,0:T(4,128)S(1)} %bitcast.10, f32[1,128]{1,0:T(1,128)S(1)} %bitcast.14, ...), custom_call_target="tpu_custom_call" | custom-call | tf_op jit(solution)/shard_map/pallas_call | solution.py:356
  87.0 0.6 copy.16
  87.6 0.5 copy.17
  88.1 0.6 copy.18
Async XLA Ops:
  0.6 0.7 copy-start.5
  0.6 0.7 copy-start.4
  0.7 0.7 copy-start.3
  0.7 0.7 copy-start.2
  0.7 0.7 copy-start.6
  1.4 0.9 %copy-start = (f32[512,128]{1,0:T(8,128)S(1)}, f32[512,128]{1,0:T(8,128)}, u32[]{:S(2)}) copy-start(f32[512,128]{1,0:T(8,128)} %inputs.1) | copy-start | bytes 786436
  2.3 0.9 %copy-start.1 = (f32[512,128]{1,0:T(8,128)S(1)}, f32[512,128]{1,0:T(8,128)}, u32[]{:S(2)}) copy-start(f32[512,128]{1,0:T(8,128)} %tests.1) | copy-start | bytes 786436
  3.3 0.7 copy-start.7
  3.9 0.7 copy-start.8
  4.6 0.7 copy-start.9

commit v2 on v1

--- a/solution.py
+++ b/solution.py
@@ -16,7 +16,8 @@
 MESH = pl.DeviceIdType.MESH
 F32 = jnp.float32
 
-RS1, Z1, AG1, SLC, SLR, Z2, AG2, Z3, P3 = range(9)
+RS1, Z1, AG1, SLC, SIB, SLR, SLR2, Z2, AG2, Z3, P3 = range(11)
+RADIX = 4
 
 
 def iota(shape, axis):
@@ -49,11 +50,13 @@
     return mm_nt(ones, a * a)[0:1, :]
 
 
-def eliminate(a, lane):
-    top = a[0:8, :]
-    cols = [jnp.broadcast_to(top[:, m : m + 1], (8, LANES)) for m in range(8)]
+def eliminate(ref, b, lane):
+    o = 8 * b
+    inside = (lane >= o) & (lane < o + 8)
+    top = ref[o : o + 8, :]
+    cols = [jnp.broadcast_to(top[:, o + m : o + m + 1], (8, LANES)) for m in range(8)]
     d = [[cols[m][i : i + 1, :] for m in range(8)] for i in range(8)]
-    rows = [jnp.where(lane < 8, (lane == i).astype(F32), top[i : i + 1, :]) for i in range(8)]
+    rows = [jnp.where(inside, (lane == o + i).astype(F32), top[i : i + 1, :]) for i in range(8)]
     for m in range(8):
         inv = 1.0 / d[m][m]
         rows[m] = rows[m] * inv
@@ -65,22 +68,36 @@
                 rows[i] = rows[i] - f * rows[m]
                 for j in range(m + 1, 8):
                     d[i][j] = d[i][j] - f * d[m][j]
-    body = a[8:, :]
-    acc = jnp.where(lane < 8, 0.0, body)
-    for m in range(8):
-        acc = acc - body[:, m : m + 1] * rows[m]
-    out = jnp.concatenate([acc] + rows, axis=0)
-    return pltpu.roll(out, LANES - 8, axis=1)
+    for t in range(1, NP // 8):
+        k = 8 * ((b + t) % (NP // 8))
+        body = ref[k : k + 8, :]
+        acc = jnp.where(inside, 0.0, body)
+        for m in range(8):
+            acc = acc - body[:, o + m : o + m + 1] * rows[m]
+        ref[k : k + 8, :] = acc
+    ref[o : o + 8, :] = jnp.concatenate(rows, axis=0)
+
+
+def eliminate_loop(ref, lane):
+    def step(_, carry):
+        for b in range(4):
+            eliminate(ref, b, lane)
+        x = pltpu.roll(ref[...], LANES - 32, axis=1)
+        ref[...] = jnp.concatenate([x[32:], x[:32]], axis=0)
+        return carry
+
+    lax.fori_loop(0, NP // 32, step, 0)
 
 
 def kernel(
     nr, nc,
+    pivots_h, tasks_sh, inputs_h, tasks_h, targets_h, il_h, tfac_h, tdiag_h, noise_h, tests_h, ttasks_h,
+    res_o, ln_o, tc_o,
     pivots, tasks_s, inputs, tasks, targets, il, tfac, tdiag, noise, tests, ttasks,
-    res_o, ln_o, tc_o,
     psrc, rsbuf, zsrc1, zbuf1, apiv, agsrc1, slsrc, bufc, bufr,
     zsrc2, zbuf2, agsrc2, gram, zsrc3, zbuf3, psrc3, pbuf3,
     art, kmat, gt_c, gt_r, kp_own, mmat, pmat,
-    ssem, rsem,
+    ssem, rsem, lsem,
 ):
     r = lax.axis_index("row")
     c = lax.axis_index("col")
@@ -101,6 +118,17 @@
     def in_col(k):
         return lax.rem(c + k, nc)
 
+    loads = [
+        pltpu.make_async_copy(src, dst, lsem.at[i])
+        for i, (src, dst) in enumerate([
+            (pivots_h, pivots), (tasks_sh, tasks_s), (inputs_h, inputs), (il_h, il), (tasks_h, tasks),
+            (targets_h, targets), (tfac_h, tfac), (tdiag_h, tdiag), (noise_h, noise), (ttasks_h, ttasks),
+            (tests_h, tests),
+        ])
+    ]
+    for load in loads:
+        load.start()
+
     order_z = sorted(range(1, nc), key=lambda k: -min(k, nc - k))
     order_p = list(range(1, nr))
 
@@ -124,9 +152,16 @@
                     src_of(to), dst, ssem.at[sem], rsem.at[sem], device_id={"row": to, "col": c}, device_id_type=MESH
                 ).start()
 
+    def send_one(src, dst, sem, dev):
+        pltpu.make_async_remote_copy(
+            src, dst, ssem.at[sem], rsem.at[sem], device_id=dev, device_id_type=MESH
+        ).start()
+
     def wait(ref, sem):
         pltpu.make_async_copy(ref, ref, sem).wait()
 
+    for load in loads:
+        load.wait()
     lane = iota((1, LANES), 1)
     eye8 = iota((TASKS, TASKS), 0) == iota((TASKS, TASKS), 1)
     eye = iota((NP, NP), 0) == iota((NP, NP), 1)
@@ -151,20 +186,27 @@
     y_own = targets[0:1, 0:SUB]
     t4 = jnp.concatenate([t_own] * 4, axis=1)
     y4 = jnp.concatenate([y_own] * 4, axis=1)
-    at_r = lane // SUB == lax.rem(r, 4)
-    at_c = lane // SUB == lax.rem(c, 4)
+    core = lax.rem(r, 2)
+    slot_r = core * chunks + mine
+    groups = nc // RADIX
+    turn = lax.rem(c, RADIX)
+    slot_c = turn * groups + c // RADIX
+    at_r = lane // SUB == lax.rem(slot_r, 4)
+    at_c = lane // SUB == lax.rem(slot_c, 4)
     slsrc[SUB : SUB + 1, :] = jnp.where(at_r, t4, 0.0)
     slsrc[SUB + 1 : SUB + 2, :] = jnp.where(at_r, y4, 0.0)
     slsrc[SUB + 2 : SUB + 3, :] = jnp.where(at_c, t4, 0.0)
     slsrc[SUB + 3 : SUB + 4, :] = jnp.where(at_c, y4, 0.0)
-    bufc[r] = slsrc[...]
-    bufr[c] = slsrc[...]
+    bufc[slot_r] = slsrc[...]
+    bufr[slot_c] = slsrc[...]
     rsbuf[r] = psrc[mine]
     art[nrr:, :] = tests[...] * scale
 
     pl.semaphore_wait(bar, nr - 1 + nc - 1)
 
     send_p(lambda to: psrc.at[to // 2], rsbuf.at[r], RS1)
+    for k in range(RADIX, nc, RADIX):
+        send_one(slsrc, bufr.at[slot_c], SLR, {"row": r, "col": in_col(k)})
     wait(rsbuf.at[pl.ds(0, nr - 1)], rsem.at[RS1])
     part = rsbuf[0]
     for k in range(1, nr):
@@ -172,7 +214,7 @@
     zsrc1[...] = part
     zbuf1[c] = part
     send_z(zsrc1, zbuf1.at[c], Z1)
-    send_p(lambda to: slsrc, bufc.at[r], SLC)
+    send_p(lambda to: slsrc, bufc.at[slot_r], SLC, step=2)
     wait(zbuf1.at[pl.ds(0, nc - 1)], rsem.at[Z1])
     part = zbuf1[0]
     for k in range(1, nc):
@@ -182,9 +224,16 @@
     apiv[my_rows, :] = part[0:cr, :]
     trow = part[cr : cr + 1, :]
     send_p(lambda to: agsrc1, apiv.at[my_rows], AG1, step=2)
-    send_z(slsrc, bufr.at[c], SLR)
-
-    wait(bufc.at[pl.ds(0, nr - 1)], rsem.at[SLC])
+    wait(bufc.at[pl.ds(0, chunks - 1)], rsem.at[SLC])
+    half = bufc.at[pl.ds(core * chunks, chunks)]
+    send_one(half, half, SIB, {"row": r + 1 - 2 * core, "col": c})
+    wait(bufr.at[pl.ds(0, groups - 1)], rsem.at[SLR])
+    kin = bufr.at[pl.ds(turn * groups, groups)]
+    for k in (1, nc - 1):
+        send_one(kin, kin, SLR2, {"row": r, "col": in_col(k)})
+    send_one(kin, kin, SLR2, {"row": r, "col": in_col(2 + (nc - 4) * lax.rem(c, 2))})
+
+    wait(bufc.at[pl.ds(0, chunks)], rsem.at[SIB])
 
     def pieces(buf, n, at):
         out = []
@@ -219,7 +268,7 @@
     eye_f = eye.astype(F32)
     fast = lax.Precision.DEFAULT
     w = (2.0 * eye_f - pm * nu) * nu
-    for _ in range(3):
+    for _ in range(4):
         w = mm(w, 2.0 * eye_f - mm(pm, w, fast), fast)
     w_t = w.T
     gtc = mm(w_t, tile_p(a_c, hs_c, ohc))
@@ -233,25 +282,24 @@
     zbuf2[c] = part
 
     send_z(zsrc2, zbuf2.at[c], Z2)
-    wait(bufr.at[pl.ds(0, nc - 1)], rsem.at[SLR])
+    oh_c = jnp.concatenate([jnp.transpose(ohc[:, k * LANES : (k + 1) * LANES]) for k in range(pcc)], axis=0)
+    cov_c = mm(oh_c, cov)
+    hs_cc = 0.5 * jnp.sum(a_c * a_c, axis=1, keepdims=True)
+
+    def k_tile(at, a, oh):
+        n = a.shape[0]
+        kmat[:, at : at + n] = jnp.exp(mm_nt(a_c, a) - hs_cc - half_sq_row(a)) * mm(cov_c, oh)
+
+    oht = onehot_rows(jnp.concatenate([ttasks[k : k + 1, :].astype(F32) for k in range(ntest)], axis=1))
+    k_tile(nrr, art[nrr:, :], oht)
+    wait(bufr.at[pl.ds(0, nc - groups)], rsem.at[SLR2])
     art[0:nrr, :] = bufr[:, 0:SUB, :].reshape(nrr, LANES)
     ohr = onehot_rows(jnp.concatenate(pieces(bufr, prr, SUB + 2), axis=1))
     y_r = jnp.concatenate(pieces(bufr, prr, SUB + 3), axis=1)
     d_r = jnp.sum(ohr * noise_col, axis=0, keepdims=True)
     di_r = 1.0 / d_r
     oht = onehot_rows(jnp.concatenate([ttasks[k : k + 1, :].astype(F32) for k in range(ntest)], axis=1))
-    cov_rt = mm(cov, jnp.concatenate([ohr, oht], axis=1))
-    a_rt = art[...]
-    hs_rt = half_sq_row(a_rt)
-
-    def k_chunk(k):
-        a = bufc[4 * k : 4 * k + 4, 0:SUB, :].reshape(LANES, LANES)
-        hs = 0.5 * jnp.sum(a * a, axis=1, keepdims=True)
-        oh = jnp.transpose(ohc[:, k * LANES : (k + 1) * LANES])
-        kmat[k * LANES : (k + 1) * LANES, :] = jnp.exp(mm_nt(a, a_rt) - hs - hs_rt) * mm(oh, cov_rt)
-
-    for k in range(pcc):
-        k_chunk(k)
+    k_tile(0, art[0:nrr, :], ohr)
 
     wait(zbuf2.at[pl.ds(0, nc - 1)], rsem.at[Z2])
     part = zbuf2[0]
@@ -262,22 +310,25 @@
     g = part[cr : cr + 1, :]
     yy = part[cr + 1 : cr + 2, :]
     send_p(lambda to: agsrc2, gram.at[my_rows], AG2, step=2)
-    gt_r[...] = mm(w_t, tile_p(art[0:nrr, :], hs_rt[:, 0:nrr], ohr))
+    a_r = art[0:nrr, :]
+    gt_r[...] = mm(w_t, tile_p(a_r, half_sq_row(a_r), ohr))
     a_own = inputs[...] * scale
     oho = onehot_rows(jnp.concatenate([tasks[k : k + 1, :].astype(F32) for k in range(nown)], axis=1))
     kp_own[...] = tile_p(a_own, half_sq_row(a_own), oho)
     base = mm(mm(w_t, pm), w)
     wait(gram.at[pl.ds(0, n_ag * cr)], rsem.at[AG2])
-    mmat[...] = base + gram[...]
-
-    def gj(_, carry):
-        mmat[...] = eliminate(mmat[...], lane)
-        pmat[...] = eliminate(pmat[...], lane)
-        return carry
-
-    lax.fori_loop(0, NP // 8, gj, 0)
+    m0 = base + gram[...]
+    mmat[...] = m0
+    for b in range(NP // 8):
+        eliminate(mmat, b, lane)
     minv = mmat[...]
-    x_col = jnp.sum(minv * g, axis=1, keepdims=True)
+
+    def solve(row):
+        col = jnp.sum(minv * row, axis=1, keepdims=True)
+        rest = row - jnp.sum(m0 * col, axis=0, keepdims=True)
+        return col + jnp.sum(minv * rest, axis=1, keepdims=True)
+
+    x_col = solve(g)
     x_row = diag_to_row(x_col, eye)
     gamma = yy[:, 0:1] - jnp.sum(g * x_row, axis=1, keepdims=True)
     rg = 1.0 / jnp.sqrt(gamma)
@@ -295,6 +346,7 @@
 
     send_z(zsrc3, zbuf3.at[c], Z3)
     zbuf3[c] = zsrc3[...]
+    eliminate_loop(pmat, lane)
     kp = kp_own[...]
     cov_d = jnp.sum(jnp.where(eye8, cov, 0.0), axis=1, keepdims=True)
     res = jnp.sum(oho * cov_d, axis=0, keepdims=True) - jnp.sum(mm(pmat[...], kp) * kp, axis=0, keepdims=True)
@@ -318,19 +370,21 @@
     for k in range(1, nr):
         part = part + pbuf3[k]
     alpha = part[1:2, 0:1]
-    b_col = jnp.sum(minv * part[0:1, :], axis=1, keepdims=True)
+    b_col = solve(part[0:1, :])
     ln = (w_r - jnp.sum(gtr * b_col, axis=0, keepdims=True)) * di_r - alpha * q_r
     out = jnp.zeros((1, SUB), F32)
     for k in range(nc):
-        out = out + jnp.where(c == k, ln[:, k * SUB : (k + 1) * SUB], 0.0)
+        out = out + jnp.where(slot_c == k, ln[:, k * SUB : (k + 1) * SUB], 0.0)
     ln_o[...] = out
     tc_o[...] = kq * (1.0 / jnp.sqrt(alpha))
 
     wait(rsbuf.at[pl.ds(0, nr - 1)], ssem.at[RS1])
     wait(zbuf1.at[pl.ds(0, nc - 1)], ssem.at[Z1])
     wait(apiv.at[pl.ds(0, n_ag * cr)], ssem.at[AG1])
-    wait(bufc.at[pl.ds(0, nr - 1)], ssem.at[SLC])
-    wait(bufr.at[pl.ds(0, nc - 1)], ssem.at[SLR])
+    wait(bufc.at[pl.ds(0, chunks - 1)], ssem.at[SLC])
+    wait(bufc.at[pl.ds(0, chunks)], ssem.at[SIB])
+    wait(bufr.at[pl.ds(0, groups - 1)], ssem.at[SLR])
+    wait(bufr.at[pl.ds(0, nc - groups)], ssem.at[SLR2])
     wait(zbuf2.at[pl.ds(0, nc - 1)], ssem.at[Z2])
     wait(gram.at[pl.ds(0, n_ag * cr)], ssem.at[AG2])
     wait(zbuf3.at[pl.ds(0, nc - 1)], ssem.at[Z3])
@@ -348,7 +402,14 @@
     nrr, ncc = nc * SUB, nr * SUB
     prr = nrr // LANES
     vmem = pl.BlockSpec(memory_space=pltpu.VMEM)
-    smem = pl.BlockSpec(memory_space=pltpu.SMEM)
+    hbm = pl.BlockSpec(memory_space=pltpu.HBM)
+    operands = (
+        pivots, tasks, inputs, tasks.reshape(nown, LANES), targets.reshape(nown, LANES), inv_length[None, :],
+        task_factor, task_diag[None, :], noise[None, :], test_inputs, test_tasks.reshape(ntest, LANES),
+    )
+    copies = [
+        (pltpu.SMEM if i < 2 else pltpu.VMEM)(x.shape, x.dtype) for i, x in enumerate(operands)
+    ]
 
     def buf(*shape):
         return pltpu.VMEM(shape, F32)
@@ -360,24 +421,21 @@
             jax.ShapeDtypeStruct((1, SUB), F32),
             jax.ShapeDtypeStruct((ntest, LANES), F32),
         ),
-        in_specs=[smem, smem] + [vmem] * 9,
+        in_specs=[hbm] * 11,
         out_specs=(vmem, vmem, vmem),
-        scratch_shapes=[
+        scratch_shapes=copies + [
             buf(chunks, cr + 1, LANES), buf(nr, cr + 1, LANES), buf(cr + 1, LANES), buf(nc, cr + 1, LANES),
             buf(NP, LANES), buf(cr, LANES), buf(SUB + 4, LANES), buf(nr, SUB + 4, LANES), buf(nc, SUB + 4, LANES),
             buf(cr + 2, LANES), buf(nc, cr + 2, LANES), buf(cr, LANES), buf(NP, LANES),
             buf(prr + ntest, LANES), buf(nc, prr + ntest, LANES), buf(2, LANES), buf(nr, 2, LANES),
             buf(nrr + test_dev, LANES), buf(ncc, nrr + test_dev), buf(NP, ncc), buf(NP, nrr), buf(NP, rows_dev),
             buf(NP, NP), buf(NP, NP),
-            pltpu.SemaphoreType.DMA((9,)), pltpu.SemaphoreType.DMA((9,)),
+            pltpu.SemaphoreType.DMA((11,)), pltpu.SemaphoreType.DMA((11,)), pltpu.SemaphoreType.DMA((11,)),
         ],
         compiler_params=pltpu.CompilerParams(
-            collective_id=0, has_side_effects=True, vmem_limit_bytes=40 * 1024 * 1024
+            collective_id=0, has_side_effects=True, vmem_limit_bytes=62 * 1024 * 1024
         ),
-    )(
-        pivots, tasks, inputs, tasks.reshape(nown, LANES), targets.reshape(nown, LANES), inv_length[None, :],
-        task_factor, task_diag[None, :], noise[None, :], test_inputs, test_tasks.reshape(ntest, LANES),
-    )
+    )(*operands)
     return res.reshape(rows_dev), ln.reshape(SUB), tc.reshape(test_dev)
 
 

time: 89 us -> 72.8 us (0.82)
  Pallas kernels: 81.8 us -> 69.6 us
  local copies, waits for them, and re-layouts: 6.24 us -> 2.34 us
    pallas_call x1, Pallas kernels: 81.8 us -> 69.6 us  [per_device(): pl.pallas_call(functools.partial(kernel, nr, nc), out_shape=(jax.ShapeDty...]
    unnamed x23 -> x9, local copies, waits for them, and re-layouts: 6.24 us -> 2.34 us
where the time goes in v2:
time: 72.8 us; the launch traced here: 72.6 us
  Pallas kernels  69.6 us (96%)
  local copies, waits for them, and re-layouts  2.34 us (3%)
    pallas_call x1, Pallas kernels, per_device(): pl.pallas_call(functools.partial(kernel, nr, nc), out_shape=(jax.ShapeDty...  69.6 us
    unnamed x9, local copies, waits for them, and re-layouts  2.34 us

profile of v2, /device:TPU:1, one launch (start us, length us, event | category | flops | bytes accessed | tf_op | source)
XLA Modules:
  0.0 72.6 jit_solution(10744064744490724814)
XLA Ops:
  0.6 69.6 %shard_map.121 = (f32[4,128]{1,0:T(4,128)}, f32[1,32]{1,0:T(1,128)}, f32[4,128]{1,0:T(4,128)}) custom-call(s32[2,64]{1,0:T(2,128)} %pivots_h.1, s32[512]{0:T(512)} %tasks_sh.1, f32[512,128]{1,0:T(8,128)} %inputs_h.1, s32[4,128]{1,0:T(4,128)} %bitcast.9, f32[4,128]{1,0:T(4,128)} %bitcast.10, f32[1,128]{1,0:T(1,128)} %bitcast.14, f32[8,8]{1,0:T(8,128)} %tfac_h.1, ...), custom_call_target="tpu_custom_call" | custom-call | tf_op jit(solution)/shard_map/pallas_call | solution.py:417
  70.2 0.0 copy-start.1
  70.2 0.6 copy-done.1
  70.9 0.0 copy-start.2
  70.9 0.0 copy-start
  70.9 0.6 copy.16
  71.5 0.0 copy-done.2
  71.5 0.5 copy.17
  72.0 0.0 copy-done
  72.0 0.6 copy.18
Async XLA Ops:
  70.2 0.7 copy-start.1
  70.9 0.6 copy-start.2
  70.9 1.1 %copy-start = (f32[4,128]{1,0:T(4,128)S(1)}, f32[4,128]{1,0:T(4,128)}, u32[]{:S(2)}) copy-start(f32[4,128]{1,0:T(4,128)} %get-tuple-element.8) | copy-start | bytes 6148

commit v3 on v2

--- a/solution.py
+++ b/solution.py
@@ -15,6 +15,7 @@
 HIGH = lax.Precision.HIGHEST
 MESH = pl.DeviceIdType.MESH
 F32 = jnp.float32
+BF16 = jnp.bfloat16
 
 RS1, Z1, AG1, SLC, SIB, SLR, SLR2, Z2, AG2, Z3, P3 = range(11)
 RADIX = 4
@@ -30,6 +31,27 @@
 
 def mm_nt(a, b, precision=HIGH):
     return lax.dot_general(a, b, (((1,), (1,)), ((), ())), precision=precision, preferred_element_type=F32)
+
+
+def split(a):
+    high = a.astype(BF16).astype(F32)
+    rest = a - high
+    mid = rest.astype(BF16).astype(F32)
+    return high, mid, rest - mid
+
+
+def pack_left(a):
+    high, mid, low = split(a)
+    return jnp.concatenate([high, mid, high, mid, high, low], axis=1).astype(BF16)
+
+
+def pack_right(a):
+    high, mid, low = split(a)
+    return jnp.concatenate([high, high, mid, mid, low, high], axis=1).astype(BF16)
+
+
+def cross(left, right):
+    return mm_nt(left, right, lax.Precision.DEFAULT)
 
 
 def diag_to_row(col, eye):
@@ -249,6 +271,7 @@
     di_c = 1.0 / jnp.sum(ohc * noise_col, axis=0, keepdims=True)
     a_c = bufc[:, 0:SUB, :].reshape(ncc, LANES)
     hs_c = half_sq_row(a_c)
+    left_c = pack_left(a_c)
     ohp_t = onehot_rows(trow)
     t_col = row_to_col(jnp.broadcast_to(trow, (NP, NP)), eye)
     ohp = (iota((NP, TASKS), 1).astype(F32) == t_col).astype(F32)
@@ -259,19 +282,22 @@
     ap = apiv[...]
     hs_p = 0.5 * jnp.sum(ap * ap, axis=1, keepdims=True)
 
-    def tile_p(a, hs, oh):
-        return jnp.exp(mm_nt(ap, a) - hs_p - hs) * mm(covp, oh)
-
-    pm = tile_p(ap, half_sq_row(ap), ohp_t)
+    left_p = pack_left(ap)
+    right_p = pack_right(ap)
+
+    def tile_p(dots, hs, oh):
+        return jnp.exp(dots - hs_p - hs) * mm(covp, oh)
+
+    pm = tile_p(cross(left_p, right_p), half_sq_row(ap), ohp_t)
     pmat[...] = pm
     nu = 1.0 / jnp.max(jnp.sum(jnp.abs(pm), axis=0, keepdims=True), axis=1, keepdims=True)
     eye_f = eye.astype(F32)
     fast = lax.Precision.DEFAULT
     w = (2.0 * eye_f - pm * nu) * nu
-    for _ in range(4):
+    for _ in range(3):
         w = mm(w, 2.0 * eye_f - mm(pm, w, fast), fast)
     w_t = w.T
-    gtc = mm(w_t, tile_p(a_c, hs_c, ohc))
+    gtc = mm(w_t, tile_p(cross(right_p, left_c), hs_c, ohc))
     gt_c[...] = gtc
     g_row = y_c * di_c
     left = jnp.concatenate([gt_c[my_rows, :] * di_c, jnp.broadcast_to(g_row, (8, ncc))], axis=0)
@@ -282,16 +308,19 @@
     zbuf2[c] = part
 
     send_z(zsrc2, zbuf2.at[c], Z2)
-    oh_c = jnp.concatenate([jnp.transpose(ohc[:, k * LANES : (k + 1) * LANES]) for k in range(pcc)], axis=0)
-    cov_c = mm(oh_c, cov)
+    oh3 = jnp.concatenate([ohc] * 3, axis=0)
+    oh_c = jnp.concatenate([jnp.transpose(oh3[:, k * LANES : (k + 1) * LANES]) for k in range(pcc)], axis=0).astype(BF16)
     hs_cc = 0.5 * jnp.sum(a_c * a_c, axis=1, keepdims=True)
 
-    def k_tile(at, a, oh):
+    def k_tile(at, a, right, oh):
         n = a.shape[0]
-        kmat[:, at : at + n] = jnp.exp(mm_nt(a_c, a) - hs_cc - half_sq_row(a)) * mm(cov_c, oh)
+        cov3 = jnp.concatenate(split(mm(cov, oh)), axis=0).astype(BF16)
+        task = mm(oh_c, cov3, lax.Precision.DEFAULT)
+        kmat[:, at : at + n] = jnp.exp(cross(left_c, right) - hs_cc - half_sq_row(a)) * task
 
     oht = onehot_rows(jnp.concatenate([ttasks[k : k + 1, :].astype(F32) for k in range(ntest)], axis=1))
-    k_tile(nrr, art[nrr:, :], oht)
+    a_t = art[nrr:, :]
+    k_tile(nrr, a_t, pack_right(a_t), oht)
     wait(bufr.at[pl.ds(0, nc - groups)], rsem.at[SLR2])
     art[0:nrr, :] = bufr[:, 0:SUB, :].reshape(nrr, LANES)
     ohr = onehot_rows(jnp.concatenate(pieces(bufr, prr, SUB + 2), axis=1))
@@ -299,7 +328,9 @@
     d_r = jnp.sum(ohr * noise_col, axis=0, keepdims=True)
     di_r = 1.0 / d_r
     oht = onehot_rows(jnp.concatenate([ttasks[k : k + 1, :].astype(F32) for k in range(ntest)], axis=1))
-    k_tile(0, art[0:nrr, :], ohr)
+    a_r = art[0:nrr, :]
+    right_r = pack_right(a_r)
+    k_tile(0, a_r, right_r, ohr)
 
     wait(zbuf2.at[pl.ds(0, nc - 1)], rsem.at[Z2])
     part = zbuf2[0]
@@ -310,11 +341,10 @@
     g = part[cr : cr + 1, :]
     yy = part[cr + 1 : cr + 2, :]
     send_p(lambda to: agsrc2, gram.at[my_rows], AG2, step=2)
-    a_r = art[0:nrr, :]
-    gt_r[...] = mm(w_t, tile_p(a_r, half_sq_row(a_r), ohr))
+    gt_r[...] = mm(w_t, tile_p(cross(left_p, right_r), half_sq_row(a_r), ohr))
     a_own = inputs[...] * scale
     oho = onehot_rows(jnp.concatenate([tasks[k : k + 1, :].astype(F32) for k in range(nown)], axis=1))
-    kp_own[...] = tile_p(a_own, half_sq_row(a_own), oho)
+    kp_own[...] = tile_p(cross(left_p, pack_right(a_own)), half_sq_row(a_own), oho)
     base = mm(mm(w_t, pm), w)
     wait(gram.at[pl.ds(0, n_ag * cr)], rsem.at[AG2])
     m0 = base + gram[...]
@@ -370,7 +400,7 @@
     for k in range(1, nr):
         part = part + pbuf3[k]
     alpha = part[1:2, 0:1]
-    b_col = solve(part[0:1, :])
+    b_col = jnp.sum(minv * part[0:1, :], axis=1, keepdims=True)
     ln = (w_r - jnp.sum(gtr * b_col, axis=0, keepdims=True)) * di_r - alpha * q_r
     out = jnp.zeros((1, SUB), F32)
     for k in range(nc):
@@ -389,6 +419,17 @@
     wait(gram.at[pl.ds(0, n_ag * cr)], ssem.at[AG2])
     wait(zbuf3.at[pl.ds(0, nc - 1)], ssem.at[Z3])
     wait(pbuf3.at[pl.ds(0, nr - 1)], ssem.at[P3])
+
+
+def hand_out(res_i, ln_i, tc_i, res_o, ln_o, tc_o, sem):
+    moves = [
+        pltpu.make_async_copy(src, dst, sem.at[i])
+        for i, (src, dst) in enumerate([(res_i, res_o), (ln_i, ln_o), (tc_i, tc_o)])
+    ]
+    for move in moves:
+        move.start()
+    for move in moves:
+        move.wait()
 
 
 def per_device(
@@ -436,6 +477,14 @@
             collective_id=0, has_side_effects=True, vmem_limit_bytes=62 * 1024 * 1024
         ),
     )(*operands)
+    res, ln, tc = pl.pallas_call(
+        hand_out,
+        out_shape=tuple(jax.ShapeDtypeStruct(x.shape, x.dtype) for x in (res, ln, tc)),
+        in_specs=[hbm] * 3,
+        out_specs=(hbm,) * 3,
+        scratch_shapes=[pltpu.SemaphoreType.DMA((3,))],
+        compiler_params=pltpu.CompilerParams(vmem_limit_bytes=62 * 1024 * 1024),
+    )(res, ln, tc)
     return res.reshape(rows_dev), ln.reshape(SUB), tc.reshape(test_dev)
 
 

time: 72.8 us -> 69.3 us (0.952)
  local copies, waits for them, and re-layouts: 2.34 us -> 0 us
  Pallas kernels: 69.6 us -> 68.6 us
    unnamed x9 -> x0, local copies, waits for them, and re-layouts: 2.34 us -> none
    pallas_call x1, Pallas kernels: 69.6 us -> 67.3 us  [per_device(): pl.pallas_call(functools.partial(kernel, nr, nc), out_shape=(jax.ShapeDty...]
    pallas_call x0 -> x1, Pallas kernels: none -> 1.27 us  [per_device(): pl.pallas_call(hand_out, out_shape=tuple((jax.ShapeDtypeStruct(x.shape, x...]
where the time goes in v3:
time: 69.3 us; the launch traced here: 69.2 us
  Pallas kernels  68.6 us (99%)
    pallas_call x1, Pallas kernels, per_device(): pl.pallas_call(functools.partial(kernel, nr, nc), out_shape=(jax.ShapeDty...  67.3 us

profile of v3, /device:TPU:1, one launch (start us, length us, event | category | flops | bytes accessed | tf_op | source)
XLA Modules:
  0.0 69.2 jit_solution(8007395831574680654)
XLA Ops:
  0.6 67.3 %shard_map.121 = (f32[4,128]{1,0:T(4,128)}, f32[1,32]{1,0:T(1,128)}, f32[4,128]{1,0:T(4,128)}) custom-call(s32[2,64]{1,0:T(2,128)} %pivots_h.1, s32[512]{0:T(512)} %tasks_sh.1, f32[512,128]{1,0:T(8,128)} %inputs_h.1, s32[4,128]{1,0:T(4,128)} %bitcast.9, f32[4,128]{1,0:T(4,128)} %bitcast.10, f32[1,128]{1,0:T(1,128)} %bitcast.12, f32[8,8]{1,0:T(8,128)} %tfac_h.1, ...), custom_call_target="tpu_custom_call" | custom-call | tf_op jit(solution)/shard_map/pallas_call | solution.py:458
  67.9 1.3 %shard_map.122 = (f32[4,128]{1,0:T(4,128)}, f32[1,32]{1,0:T(1,128)}, f32[4,128]{1,0:T(4,128)}) custom-call(f32[4,128]{1,0:T(4,128)} %get-tuple-element.9.res_i, f32[1,32]{1,0:T(1,128)} %get-tuple-element.10.ln_i, f32[4,128]{1,0:T(4,128)} %get-tuple-element.11.tc_i), custom_call_target="tpu_custom_call" | custom-call | tf_op jit(solution)/shard_map/pallas_call | solution.py:480
